TPU v7x, 32 devices: a whole 2x2x4 slice. The times are simulated.
32 devices in a mesh: groups: 2 (over x), blk: 16 (over z, y, core).
Axes of the slice: x: 2, y: 2, z: 4, core: 2. Of those that a mesh axis runs over, the one named last changes fastest.
Arguments:
- hidden: bfloat16 [12288, 5120], P(('groups', 'blk')), parts along dimension 0, may hold values from -6 to 6
- norm_gain: float32 [5120], replicated, may hold values from 0.5 to 1.5
- q_weight: bfloat16 [5120, 2560], P('blk'), may hold values from -0.078125 to 0.078125
- q_bias: float32 [2560], replicated, may hold values from -5 to 5
- kv_store: bfloat16 [128, 2, 512, 512], P(('groups', 'blk')), parts along dimension 0, may hold values from -620 to 620
- block_home: int32 [128], P('groups'), parts along dimension 0, may hold values from 0 to 63, as said below
- need_ids: int32 [64, 2], P(('groups', 'blk')), parts along dimension 0, may hold values from 0 to 63, as said below
- hole_pos: int32 [64], P(('groups', 'blk')), parts along dimension 0, may hold values from 0 to 32767, as said below
- fill_len: int32 [64], P(('groups', 'blk')), parts along dimension 0, may hold values from 48 to 192
Outputs:
- attended: bfloat16 [12288, 2560], P(('groups', 'blk')), parts along dimension 0
There are 2 independent parts, one for each index of `groups`. A program takes and returns all parts, laid end to end along the dimension named above; an argument that names none is the same for every part. Nothing has to cross between parts.
Inputs may be any that keep to these rules, and one draw needn't show every extreme that they name: block_home is a permutation; block b is kept by device block_home[b] // 4 of blk. `need_ids`: the 4 blocks listed by the candidates of one device of blk are all different and are kept by different devices, each at most 2 places away from it along blk, counted around the loop. The span from hole_pos to hole_pos + fill_len - 1 lies inside the first block that the candidate lists.
All inputs are finite; a program needn't handle non-finite values.
Results may differ from a plain program's by a relative error of at most 0.0035.
The roundings to bfloat16 on the way count: a program that leaves them out, or rounds other values in their place, can miss the bound.
Values may be sent and summed in bfloat16 or wider, within the bound.
A program may use at most 128 MiB of HBM per device.

v0:
```python
import math
import jax
import jax.numpy as jnp
from jax import lax
from jax.sharding import PartitionSpec as P

HEAD_SIZE = 128
QUERY_HEADS = 20
KEY_HEADS = 4
BLOCK_TOKENS = 512
BLOCKS_NEEDED = 2
REACH = 2


def passed_along(block, axis, distance):
    devices = range(lax.axis_size(axis))
    route = [((i - distance) % len(devices), i) for i in devices]
    return lax.ppermute(block, axis, route)


def rms_normed(hidden, norm_gain):
    widened = hidden.astype(jnp.float32)
    scale_inv = lax.rsqrt(jnp.mean(widened * widened, axis=-1, keepdims=True) + 1e-06)
    return (widened * scale_inv * norm_gain).astype(jnp.bfloat16)


def attend_single(packed):
    candidate_query_rows, sketch_blocks, block_ids, hole_start, fill_rows = packed
    count_of_rows = candidate_query_rows.shape[0]
    block_key_rows = sketch_blocks[:, 0].reshape(BLOCKS_NEEDED * BLOCK_TOKENS, KEY_HEADS, HEAD_SIZE)
    block_value_rows = sketch_blocks[:, 1].reshape(
        BLOCKS_NEEDED * BLOCK_TOKENS, KEY_HEADS, HEAD_SIZE
    )
    query_matrix = candidate_query_rows.reshape(
        count_of_rows, KEY_HEADS, QUERY_HEADS // KEY_HEADS, HEAD_SIZE
    )
    scores = jnp.einsum(
        "rkgd,tkd->rkgt", query_matrix, block_key_rows, preferred_element_type=jnp.float32
    ) / math.sqrt(HEAD_SIZE)
    position = (
        block_ids[:, None] * BLOCK_TOKENS + jnp.arange(BLOCK_TOKENS, dtype=jnp.int32)[None, :]
    ).reshape(BLOCKS_NEEDED * BLOCK_TOKENS)
    masked = (position >= hole_start) & (position < hole_start + fill_rows)
    scores = jnp.where(masked[None, None, None, :], jnp.float32(-1e30), scores)
    row_max = jnp.max(scores, axis=-1, keepdims=True)
    exponent = jnp.exp(scores - row_max)
    denominator = jnp.sum(exponent, axis=-1)
    weights = exponent.astype(jnp.bfloat16)
    attended = (
        jnp.einsum("rkgt,tkd->rkgd", weights, block_value_rows, preferred_element_type=jnp.float32)
        / denominator[..., None]
    )
    attended = attended.reshape(count_of_rows, QUERY_HEADS * HEAD_SIZE)
    live_rows = jnp.arange(count_of_rows, dtype=jnp.int32) < fill_rows
    return jnp.where(live_rows[:, None], attended, jnp.float32(0.0)).astype(jnp.bfloat16)


def attend_all(query, sketch_blocks, block_lists, hole_starts, fill_rows):
    cand_count = block_lists.shape[0]
    count_of_rows = query.shape[0] // cand_count
    shaped = query.reshape(cand_count, count_of_rows, QUERY_HEADS * HEAD_SIZE)
    results = lax.map(attend_single, (shaped, sketch_blocks, block_lists, hole_starts, fill_rows))
    return results.reshape(cand_count * count_of_rows, QUERY_HEADS * HEAD_SIZE)


def shards(hidden, norm_gain, q_weight, q_bias, kv_store, block_home, need_ids, hole_pos, fill_len):
    normed = rms_normed(hidden, norm_gain)
    whole_weight = lax.all_gather(q_weight, "blk", axis=0, tiled=True)
    projected = jnp.dot(normed, whole_weight, preferred_element_type=jnp.float32)
    query = (projected + q_bias).astype(jnp.bfloat16)
    device_count = lax.axis_size("blk")
    myself = lax.axis_index("blk")
    local_count = kv_store.shape[0]
    empty_block = jnp.zeros(kv_store.shape[1:], kv_store.dtype)

    def select_block(block_lists):
        stored_at = block_home[block_lists.reshape(-1)]
        owned_here = stored_at // local_count == myself
        slot_index = jnp.sum(jnp.where(owned_here, stored_at % local_count, 0))
        has_block = jnp.any(owned_here)
        chosen = lax.dynamic_index_in_dim(kv_store, slot_index, 0, keepdims=False)
        return jnp.where(has_block, chosen, empty_block)

    incoming = []
    for offset in range(-REACH, REACH + 1):
        if offset == 0:
            incoming.append(select_block(need_ids))
        else:
            asked = passed_along(need_ids, "blk", -offset)
            incoming.append(passed_along(select_block(asked), "blk", offset))
    arrived = jnp.stack(incoming, axis=0)
    owners = block_home[need_ids] // local_count
    slot_of_entry = jnp.remainder(myself - owners + REACH, device_count)
    sketch_blocks = jnp.take(arrived, slot_of_entry, axis=0)
    return attend_all(query, sketch_blocks, need_ids, hole_pos, fill_len)


def solution(mesh):
    placed = (
        P(("groups", "blk"), None),
        P(),
        P("blk", None),
        P(),
        P(("groups", "blk"), None, None, None),
        P("groups"),
        P(("groups", "blk"), None),
        P(("groups", "blk")),
        P(("groups", "blk")),
    )
    return jax.shard_map(
        shards, mesh=mesh, in_specs=placed, out_specs=P(("groups", "blk"), None), check_vma=False
    )
```

profile of v0, /device:TPU:0, one launch (start us, length us, event | category | flops | bytes accessed | tf_op | source)
XLA Modules:
  0.0 285.8 jit_solution(10790405811085733742)
XLA Ops:
  6.5 0.7 all-gather.2.cloned.1.call-update
  7.8 2.6 collective-permute-start
  10.3 4.1 %collective-permute-start.4 = (s32[2,2]{1,0:T(2,128)}, s32[2,2]{1,0:T(2,128)S(1)}, u32[]{:S(2)}, u32[]{:S(2)}) collective-permute-start(s32[2,2]{1,0:T(2,128)} %param.17), channel_id=1, source_target_pairs={{1,0},{2,1},{3,2},{4,3},{5,4},{6,5},{7,6},{8,7},{9,8},{10,9},{11,1... | collective-permute-start | bytes 56 | tf_op jit(solution)/shard_map/ppermute | solution.py:18
  15.1 0.8 reshape.363
  15.9 0.7 compare_select_fusion.2
  18.7 0.7 fusion.31
  22.4 0.6 gather_fusion.1
  23.0 0.7 compare_reduce_fusion.3
  23.7 0.7 fusion.29
  25.7 0.7 fusion.30
  29.1 4.0 %select_bitcast_fusion.2 = (bf16[2,512,512]{2,1,0:T(8,128)(2,1)S(1)}, bf16[2,512,512]{2,1,0:T(8,128)(2,1)}) fusion(bf16[4,2,512,512]{3,2,1,0:T(8,128)(2,1)} %param.15, s32[]{:T(128)S(6)} %select_n.257, pred[]{:T(512)} %get-tuple-element.77, s32[]{:T(128)S(6)} %select_n.249, pred[]{:T(512)} %get-tuple-element.92), kind=kLoop, calls=%fused_computation.48 | loop fusion | flops 1048576 | bytes 4194314 | tf_op jit(solution)/shard_map/jit(_where)/select_n | solution.py:82
  33.1 2.8 collective-permute-start.1
  37.3 0.7 compare_reduce_fusion
  39.8 0.7 fusion.33
  43.1 38.2 %collective-permute-done.1 = bf16[2,512,512]{2,1,0:T(8,128)(2,1)S(1)} collective-permute-done((bf16[2,512,512]{2,1,0:T(8,128)(2,1)}, bf16[2,512,512]{2,1,0:T(8,128)(2,1)S(1)}, u32[]{:S(2)}, u32[]{:S(2)}) %collective-permute-start.1) | collective-permute-done | bytes 1048608 | tf_op jit(solution)/shard_map/ppermute | solution.py:18
  81.3 33.3 %collective-permute-done.3 = bf16[2,512,512]{2,1,0:T(8,128)(2,1)S(1)} collective-permute-done((bf16[2,512,512]{2,1,0:T(8,128)(2,1)S(1)}, bf16[2,512,512]{2,1,0:T(8,128)(2,1)S(1)}, u32[]{:S(2)}, u32[]{:S(2)}) %collective-permute-start.3) | collective-permute-done | bytes 1048608 | tf_op jit(solution)/shard_map/ppermute | solution.py:18
  114.7 2.4 select_bitcast_fusion
  117.1 2.4 copy-done.4
  120.1 1.2 collective-permute-start.7
  121.4 3.0 %fusion.15 = f32[384]{0:T(512)S(1)} fusion(bf16[384,5120]{1,0:T(8,128)(2,1)} %param.11), kind=kLoop, calls=%fused_computation.33 | loop fusion | flops 5897856 | bytes 3933696 | tf_op jit(solution)/shard_map/reduce_sum | solution.py:23
  124.5 45.0 %collective-permute-done.5 = bf16[2,512,512]{2,1,0:T(8,128)(2,1)S(1)} collective-permute-done((bf16[2,512,512]{2,1,0:T(8,128)(2,1)S(1)}, bf16[2,512,512]{2,1,0:T(8,128)(2,1)S(1)}, u32[]{:S(2)}, u32[]{:S(2)}) %collective-permute-start.5) | collective-permute-done | bytes 1048608 | tf_op jit(solution)/shard_map/ppermute | solution.py:18
  169.4 1.1 bitcast_dynamic-update-slice_fusion.1
  170.5 0.7 collective-permute-done.7
  171.2 1.0 bitcast_dynamic-update-slice_fusion
  172.3 5.3 %gather_fusion.6 = bf16[4,2,512,512]{3,2,1,0:T(8,128)(2,1)} fusion(bf16[5,2,512,512]{3,2,1,0:T(8,128)(2,1)} %bitcast_dynamic-update-slice_fusion, s32[1024]{0:T(1024)S(1)} %pad_clamp_fusion), kind=kCustom, calls=%fused_computation.6 | custom fusion | bytes 8388624 | tf_op jit(solution)/shard_map/jit(_take)/gather | solution.py:94
  177.6 4.7 %broadcast_select_fusion = bf16[2,2,2,512,512]{4,3,2,1,0:T(8,128)(2,1)} fusion(bf16[2,2,2,512,512]{4,3,2,1,0:T(8,128)(2,1)} %bitcast.95, pred[2,2]{1,0:T(4,128)(4,1)S(1)} %compare_and_fusion.1), kind=kLoop, calls=%fused_computation.38 | loop fusion | flops 2097152 | bytes 8388612 | tf_op jit(solution)/shard_map/jit(_take)/select_n | solution.py:94
  182.3 30.0 %all-gather.2.cloned.1.call-done = bf16[5120,2560]{1,0:T(8,128)(2,1)} async-done(((bf16[320,2560]{1,0:T(8,128)(2,1)}), bf16[5120,2560]{1,0:T(8,128)(2,1)}) %all-gather.2.cloned.1.call-update) | async-done | bytes 26214416 | tf_op jit(solution)/shard_map/all_gather | solution.py:68
  212.3 17.5 %fusion.18 = bf16[384,2560]{1,0:T(8,128)(2,1)} fusion(bf16[5120,2560]{1,0:T(8,128)(2,1)} %all-gather.2.cloned.1.call-done, bf16[384,5120]{1,0:T(8,128)(2,1)} %param.11, f32[5120]{0:T(1024)S(1)} %copy-done.6, f32[384]{0:T(512)S(1)} %add_rsqrt_fusion, f32[2560]{0:T(1024)S(1)} %copy-done.7), kind=kOutput, calls=%fused_computation.37 | convolution fusion | flops 10076160000 | bytes 32144896 | tf_op jit(solution)/shard_map/dot_general | solution.py:69
  229.8 48.5 %while.10 = (s32[]{:T(128)}, bf16[2,192,2560]{2,1,0:T(8,128)(2,1)}, s32[2]{0:T(128)S(1)}, bf16[2,2,2,512,512]{4,3,2,1,0:T(8,128)(2,1)}, s32[2,2]{1,0:T(2,128)S(1...) while((s32[]{:T(128)}, bf16[2,192,2560]{2,1,0:T(8,128)(2,1)}, s32[2]{0:T(128)S(1)}, ...), condition=%wide.region_14.15_spmd, body=%wide.region_11.14_spmd.sunk | while | flops 2057990912 | bytes 79906376 | solution.py:62
  233.5 1.3 constant_dynamic-slice_fusion.7
  235.3 1.7 copy_bitcast_fusion.2
  237.1 1.2 fusion.47
  238.3 1.3 squeeze.29
  239.6 1.1 squeeze.30
  240.8 2.9 %bitcast_reduce_fusion.2 = (f32[192,4,5]{0,2,1:T(8,128)S(1)}, f32[4,1024,192,5]{1,2,3,0:T(8,128)S(1)}) fusion(pred[1024]{0:T(1024)(128)(4,1)S(1)} %and.179, bf16[192,4,5,128]{0,3,2,1:T(8,128)(2,1)S(1)} %bitcast.91, bf16[1024,4,128,1]{2,1,0,3:T(4,128)(2,1)S(1)} %bitcast.93), kind=kOutput, calls=%fused_computation.8.clone.1 | convolution fusion | flops 1018425600 | bytes 17776640 | tf_op jit(solution)/shard_map/while/body/eval_jaxpr/rkgd,tkd->rkgt/dot_general | solution.py:37
  243.7 3.9 %fusion.48 = f32[192,4,5]{0,2,1:T(8,128)S(1)} fusion(f32[4,1024,192,5]{1,2,3,0:T(8,128)S(1)} %get-tuple-element.144, f32[192,4,5]{0,2,1:T(8,128)S(1)} %get-tuple-element.145, pred[1024]{0:T(1024)(128)(4,1)S(1)} %and.179), kind=kLoop, calls=%fused_computation.11.clone.1 | loop fusion | flops 15724800 | bytes 15760384 | tf_op jit(solution)/shard_map/while/body/eval_jaxpr/reduce_sum | solution.py:47
  247.7 3.9 %bitcast_divide_fusion.2 = bf16[192,4,5,128]{3,0,2,1:T(8,128)(2,1)S(1)} fusion(f32[4,1024,192,5]{1,2,3,0:T(8,128)S(1)} %get-tuple-element.144, f32[192,4,5]{0,2,1:T(8,128)S(1)} %get-tuple-element.145, pred[1024]{0:T(1024)(128)(4,1)S(1)} %and.179, bf16[1024,4,128,1]{2,1,0,3:T(4,128)(2,1)S(1)} %bitcast.94, f32[192,4,5]{0,2,1:T(8,128)S(1)} %fusion.48), kind=kOutput, calls=%fused_computation.17.clone.1 | convolution fusion | flops 1023344640 | bytes 17792000 | tf_op jit(solution)/shard_map/while/body/eval_jaxpr/rkgt,tkd->rkgd/dot_general | solution.py:50
  253.1 1.0 constant_dynamic-update-slice_fusion.2
  257.7 1.3 constant_dynamic-slice_fusion.7
  259.6 1.7 copy_bitcast_fusion.2
  261.3 1.2 fusion.47
  262.5 1.3 squeeze.29
  263.8 1.1 squeeze.30
  265.0 2.9 %bitcast_reduce_fusion.2 = (f32[192,4,5]{0,2,1:T(8,128)S(1)}, f32[4,1024,192,5]{1,2,3,0:T(8,128)S(1)}) fusion(pred[1024]{0:T(1024)(128)(4,1)S(1)} %and.179, bf16[192,4,5,128]{0,3,2,1:T(8,128)(2,1)S(1)} %bitcast.91, bf16[1024,4,128,1]{2,1,0,3:T(4,128)(2,1)S(1)} %bitcast.93), kind=kOutput, calls=%fused_computation.8.clone.1 | convolution fusion | flops 1018425600 | bytes 17776640 | tf_op jit(solution)/shard_map/while/body/eval_jaxpr/rkgd,tkd->rkgt/dot_general | solution.py:37
  267.9 3.9 %fusion.48 = f32[192,4,5]{0,2,1:T(8,128)S(1)} fusion(f32[4,1024,192,5]{1,2,3,0:T(8,128)S(1)} %get-tuple-element.144, f32[192,4,5]{0,2,1:T(8,128)S(1)} %get-tuple-element.145, pred[1024]{0:T(1024)(128)(4,1)S(1)} %and.179), kind=kLoop, calls=%fused_computation.11.clone.1 | loop fusion | flops 15724800 | bytes 15760384 | tf_op jit(solution)/shard_map/while/body/eval_jaxpr/reduce_sum | solution.py:47
  271.9 3.9 %bitcast_divide_fusion.2 = bf16[192,4,5,128]{3,0,2,1:T(8,128)(2,1)S(1)} fusion(f32[4,1024,192,5]{1,2,3,0:T(8,128)S(1)} %get-tuple-element.144, f32[192,4,5]{0,2,1:T(8,128)S(1)} %get-tuple-element.145, pred[1024]{0:T(1024)(128)(4,1)S(1)} %and.179, bf16[1024,4,128,1]{2,1,0,3:T(4,128)(2,1)S(1)} %bitcast.94, f32[192,4,5]{0,2,1:T(8,128)S(1)} %fusion.48), kind=kOutput, calls=%fused_computation.17.clone.1 | convolution fusion | flops 1023344640 | bytes 17792000 | tf_op jit(solution)/shard_map/while/body/eval_jaxpr/rkgt,tkd->rkgd/dot_general | solution.py:50
  277.3 1.0 constant_dynamic-update-slice_fusion.2
  278.3 0.7 copy-done.1
  (81 shorter events, 16.0 us)
Async XLA Ops:
  6.5 10.1 %copy-start = (s32[64]{0:T(128)S(1)}, s32[64]{0:T(128)}, u32[]{:S(2)}) copy-start(s32[64]{0:T(128)} %param.16) | copy-start | bytes 772
  6.5 205.8 %all-gather.2.cloned.1.call-start = ((), (), s32[]{:S(2)}) async-start(), calls=%async_computation | async-start | bytes 27852800 | tf_op jit(solution)/shard_map/all_gather | solution.py:68
  7.3 14.2 %collective-permute-start.2 = (s32[2,2]{1,0:T(2,128)}, s32[2,2]{1,0:T(2,128)S(1)}, u32[]{:S(2)}, u32[]{:S(2)}) collective-permute-start(s32[2,2]{1,0:T(2,128)} %param.17), channel_id=1, source_target_pairs={{15,0},{0,1},{1,2},{2,3},{3,4},{4,5},{5,6},{6,7},{7,8},{8,9},{9,10... | collective-permute-start | bytes 56 | tf_op jit(solution)/shard_map/ppermute | solution.py:18
  7.8 14.5 %collective-permute-start = (s32[2,2]{1,0:T(2,128)}, s32[2,2]{1,0:T(2,128)S(1)}, u32[]{:S(2)}, u32[]{:S(2)}) collective-permute-start(s32[2,2]{1,0:T(2,128)} %param.17), channel_id=1, source_target_pairs={{14,0},{15,1},{0,2},{1,3},{2,4},{3,5},{4,6},{5,7},{6,8},{7,9},{8,1... | collective-permute-start | bytes 56 | tf_op jit(solution)/shard_map/ppermute | solution.py:18
  10.3 25.5 %collective-permute-start.4 = (s32[2,2]{1,0:T(2,128)}, s32[2,2]{1,0:T(2,128)S(1)}, u32[]{:S(2)}, u32[]{:S(2)}) collective-permute-start(s32[2,2]{1,0:T(2,128)} %param.17), channel_id=1, source_target_pairs={{1,0},{2,1},{3,2},{4,3},{5,4},{6,5},{7,6},{8,7},{9,8},{10,9},{11,1... | collective-permute-start | bytes 56 | tf_op jit(solution)/shard_map/ppermute | solution.py:18
  14.4 22.1 %collective-permute-start.6 = (s32[2,2]{1,0:T(2,128)}, s32[2,2]{1,0:T(2,128)S(1)}, u32[]{:S(2)}, u32[]{:S(2)}) collective-permute-start(s32[2,2]{1,0:T(2,128)} %param.17), channel_id=1, source_target_pairs={{2,0},{3,1},{4,2},{5,3},{6,4},{7,5},{8,6},{9,7},{10,8},{11,9},{12,... | collective-permute-start | bytes 56 | tf_op jit(solution)/shard_map/ppermute | solution.py:18
  33.1 48.2 %collective-permute-start.1 = (bf16[2,512,512]{2,1,0:T(8,128)(2,1)}, bf16[2,512,512]{2,1,0:T(8,128)(2,1)S(1)}, u32[]{:S(2)}, u32[]{:S(2)}) collective-permute-start(bf16[2,512,512]{2,1,0:T(8,128)(2,1)} %get-tuple-element.89), channel_id=1, source_target_pairs={{2,0},{3,1},{4,2},{5,3},{6,4},{7,5},{8,6},{9,7},{10,8},{11,9},{12,... | collective-permute-start | bytes 3145736 | tf_op jit(solution)/shard_map/ppermute | solution.py:18
  36.6 78.1 %collective-permute-start.3 = (bf16[2,512,512]{2,1,0:T(8,128)(2,1)S(1)}, bf16[2,512,512]{2,1,0:T(8,128)(2,1)S(1)}, u32[]{:S(2)}, u32[]{:S(2)}) collective-permute-start(bf16[2,512,512]{2,1,0:T(8,128)(2,1)S(1)} %get-tuple-element.88), channel_id=1, source_target_pairs={{1,0},{2,1},{3,2},{4,3},{5,4},{6,5},{7,6},{8,7},{9,8},{10,9},{11,1... | collective-permute-start | bytes 3145736 | tf_op jit(solution)/shard_map/ppermute | solution.py:18
  43.1 71.7 %copy-start.3 = (bf16[4,2,512,512]{3,2,1,0:T(8,128)(2,1)S(1)}, bf16[4,2,512,512]{3,2,1,0:T(8,128)(2,1)}, u32[]{:S(2)}) copy-start(bf16[4,2,512,512]{3,2,1,0:T(8,128)(2,1)} %param.15) | copy-start | bytes 12582916
  117.1 2.4 copy-start.4
  119.5 49.9 %collective-permute-start.5 = (bf16[2,512,512]{2,1,0:T(8,128)(2,1)S(1)}, bf16[2,512,512]{2,1,0:T(8,128)(2,1)S(1)}, u32[]{:S(2)}, u32[]{:S(2)}) collective-permute-start(bf16[2,512,512]{2,1,0:T(8,128)(2,1)S(1)} %get-tuple-element.87), channel_id=1, source_target_pairs={{15,0},{0,1},{1,2},{2,3},{3,4},{4,5},{5,6},{6,7},{7,8},{8,9},{9,10... | collective-permute-start | bytes 3145736 | tf_op jit(solution)/shard_map/ppermute | solution.py:18
  120.1 51.1 %collective-permute-start.7 = (bf16[2,512,512]{2,1,0:T(8,128)(2,1)S(1)}, bf16[2,512,512]{2,1,0:T(8,128)(2,1)S(1)}, u32[]{:S(2)}, u32[]{:S(2)}) collective-permute-start(bf16[2,512,512]{2,1,0:T(8,128)(2,1)S(1)} %get-tuple-element.85), channel_id=1, source_target_pairs={{14,0},{15,1},{0,2},{1,3},{2,4},{3,5},{4,6},{5,7},{6,8},{7,9},{8,1... | collective-permute-start | bytes 3145736 | tf_op jit(solution)/shard_map/ppermute | solution.py:18
  177.6 34.8 %copy-start.6 = (f32[5120]{0:T(1024)S(1)}, f32[5120]{0:T(1024)}, u32[]{:S(2)}) copy-start(f32[5120]{0:T(1024)} %param.12) | copy-start | bytes 61444
  177.6 34.8 %copy-start.7 = (f32[2560]{0:T(1024)S(1)}, f32[2560]{0:T(1024)}, u32[]{:S(2)}) copy-start(f32[2560]{0:T(1024)} %param.14) | copy-start | bytes 30724
  182.3 47.5 %copy-start.5 = (s32[2,2]{1,0:T(2,128)S(1)}, s32[2,2]{1,0:T(2,128)}, u32[]{:S(2)}) copy-start(s32[2,2]{1,0:T(2,128)} %param.17) | copy-start | bytes 52
  182.3 47.5 %copy-start.8 = (s32[2]{0:T(128)S(1)}, s32[2]{0:T(128)}, u32[]{:S(2)}) copy-start(s32[2]{0:T(128)} %param.19) | copy-start | bytes 28
  182.3 47.5 %copy-start.9 = (s32[2]{0:T(128)S(1)}, s32[2]{0:T(128)}, u32[]{:S(2)}) copy-start(s32[2]{0:T(128)} %param.18) | copy-start | bytes 28
  243.7 4.0 %copy-start.2 = (bf16[1024,4,128]{2,1,0:T(4,128)(2,1)S(1)}, bf16[1024,4,128]{2,1,0:T(4,128)(2,1)}, u32[]{:S(2)}) copy-start(bf16[1024,4,128]{2,1,0:T(4,128)(2,1)} %squeeze.30) | copy-start | bytes 3145732 | tf_op jit(solution)/shard_map/while
  267.9 4.0 %copy-start.2 = (bf16[1024,4,128]{2,1,0:T(4,128)(2,1)S(1)}, bf16[1024,4,128]{2,1,0:T(4,128)(2,1)}, u32[]{:S(2)}) copy-start(bf16[1024,4,128]{2,1,0:T(4,128)(2,1)} %squeeze.30) | copy-start | bytes 3145732 | tf_op jit(solution)/shard_map/while
  278.3 0.7 copy-start.1
Sparse Core Ops, SparseCore 0:
  9.0 203.3 all-gather.1
where the time goes:
time: 287 us; the launch traced here: 286 us
  waiting for transfers between devices  148 us (52%)
  local copies, waits for them, and re-layouts  37.2 us (13%)
  other arithmetic  31.4 us (11%)
  matrix products  31.2 us (11%)
  between operations  23.2 us (8%)
  starting transfers between devices  12.4 us (4%)
    ppermute x8, waiting for transfers between devices, passed_along(): return lax.ppermute(block, axis, route)  117 us
    all_gather x1, waiting for transfers between devices, shards(): whole_weight = lax.all_gather(q_weight, 'blk', axis=0, tiled=True)  30 us
    dot_general x1, matrix products, shards(): jnp.dot(normed, whole_weight, preferred_element_type=jnp.float32)  17.5 us
    ppermute x8, starting transfers between devices, passed_along(): return lax.ppermute(block, axis, route)  12.3 us
    reduce_sum x2, other arithmetic, attend_single(): denominator = jnp.sum(exponent, axis=-1)  7.9 us
    dot_general x2, matrix products, attend_single(): jnp.einsum('rkgt,tkd->rkgd', weights, block_value_rows, preferred_element...  7.83 us
    select_n x2, other arithmetic, select_block(): return jnp.where(has_block, chosen, empty_block)  6.33 us
    dynamic_slice x8, local copies, waits for them, and re-layouts, attend_all(): lax.map(attend_single, (shaped, sketch_blocks, block_lists, hole_starts,...  6.01 us
  transfers between devices with their start and end apart: 9, of which 5 were waited for; matrix products, arithmetic and copies ran while one was open for 12% of the time, Pallas kernels for 0%

commit v1 on v0

--- a/solution.py
+++ b/solution.py
@@ -3,6 +3,7 @@
 import jax.numpy as jnp
 from jax import lax
 from jax.sharding import PartitionSpec as P
+from jax.lax import axis_index, axis_size, ppermute
 
 HEAD_SIZE = 128
 QUERY_HEADS = 20
@@ -64,8 +65,34 @@
 
 
 def shards(hidden, norm_gain, q_weight, q_bias, kv_store, block_home, need_ids, hole_pos, fill_len):
+
+    def lead_the_inputs(z):
+        mesh_ax = "blk"
+        v1, fresh, piece_out = (axis_size(mesh_ax), axis_index(mesh_ax), z.shape[0])
+        samples = []
+        for w in range(v1):
+            samples.append((w, (w + 1) % v1))
+        tray = []
+        for w in range(v1):
+            tray.append((w, (w - 1) % v1))
+        val = jnp.zeros((*z.shape[:0], v1 * piece_out, *z.shape[1:]), z.dtype)
+        val = lax.dynamic_update_slice_in_dim(val, z, fresh * piece_out, axis=0)
+        spare = r_now = z
+        z2 = v1 // 2
+        for dev_j in range(1, z2 + 1):
+            spare = ppermute(spare, axis_name=mesh_ax, perm=samples)
+            val = lax.dynamic_update_slice_in_dim(
+                val, spare, (fresh - dev_j) % v1 * piece_out, axis=0
+            )
+            if dev_j < v1 - z2:
+                r_now = ppermute(r_now, mesh_ax, perm=tray)
+                val = lax.dynamic_update_slice_in_dim(
+                    val, r_now, (fresh + dev_j) % v1 * piece_out, axis=0
+                )
+        return val
+
     normed = rms_normed(hidden, norm_gain)
-    whole_weight = lax.all_gather(q_weight, "blk", axis=0, tiled=True)
+    whole_weight = lead_the_inputs(q_weight)
     projected = jnp.dot(normed, whole_weight, preferred_element_type=jnp.float32)
     query = (projected + q_bias).astype(jnp.bfloat16)
     device_count = lax.axis_size("blk")

time: 287 us -> 430 us (1.50)
  the two profiles are of different devices: /device:TPU:0 before, /device:TPU:1 now
where the time goes in v1:
time: 430 us; the launch traced here: 429 us
  waiting for transfers between devices  239 us (56%)
  local copies, waits for them, and re-layouts  82.3 us (19%)
  matrix products  36.5 us (8%)
  other arithmetic  33.4 us (8%)
  starting transfers between devices  25.2 us (6%)
  between operations  9.85 us (2%)
    ppermute x8, waiting for transfers between devices, lead_the_inputs(): spare = ppermute(spare, axis_name=mesh_ax, perm=samples)  116 us
    ppermute x7, waiting for transfers between devices, lead_the_inputs(): r_now = ppermute(r_now, mesh_ax, perm=tray)  108 us
    ppermute x8, starting transfers between devices, lead_the_inputs(): spare = ppermute(spare, axis_name=mesh_ax, perm=samples)  16.6 us
    dynamic_update_slice x8, local copies, waits for them, and re-layouts, lead_the_inputs(): lax.dynamic_update_slice_in_dim(val, spare, (fresh - dev_j) % v1 * piece_...  16.1 us
    dot_general x1, matrix products, shards(): jnp.dot(normed, whole_weight, preferred_element_type=jnp.float32)  15.6 us
    dot_general x2, matrix products, attend_single(): jnp.einsum('rkgt,tkd->rkgd', weights, block_value_rows, preferred_element...  15 us
    dynamic_update_slice x7, local copies, waits for them, and re-layouts, lead_the_inputs(): lax.dynamic_update_slice_in_dim(val, r_now, (fresh + dev_j) % v1 * piece_...  14.9 us
    ppermute x8, waiting for transfers between devices, passed_along(): return lax.ppermute(block, axis, route)  14.6 us
  transfers between devices with their start and end apart: 23, of which 14 were waited for; matrix products, arithmetic and copies ran while one was open for 19% of the time, Pallas kernels for 0%

profile of v1, /device:TPU:1, one launch (start us, length us, event | category | flops | bytes accessed | tf_op | source)
XLA Modules:
  0.0 428.6 jit_solution(3161124584141743834)
XLA Ops:
  0.0 2.6 collective-permute-start.8
  2.6 35.9 %collective-permute-done.8 = bf16[320,2560]{1,0:T(8,128)(2,1)} collective-permute-done((bf16[320,2560]{1,0:T(8,128)(2,1)}, bf16[320,2560]{1,0:T(8,128)(2,1)}, u32[]{:S(2)}, u32[]{:S(2)}) %collective-permute-start.8) | collective-permute-done | bytes 1638432 | tf_op jit(solution)/shard_map/ppermute | solution.py:83
  38.6 2.5 collective-permute-start.10
  44.7 13.8 %collective-permute-done.9 = bf16[320,2560]{1,0:T(8,128)(2,1)S(1)} collective-permute-done((bf16[320,2560]{1,0:T(8,128)(2,1)}, bf16[320,2560]{1,0:T(8,128)(2,1)S(1)}, u32[]{:S(2)}, u32[]{:S(2)}) %collective-permute-start.9) | collective-permute-done | bytes 1638432 | tf_op jit(solution)/shard_map/ppermute | solution.py:88
  59.2 17.8 %collective-permute-done.10 = bf16[320,2560]{1,0:T(8,128)(2,1)S(1)} collective-permute-done((bf16[320,2560]{1,0:T(8,128)(2,1)}, bf16[320,2560]{1,0:T(8,128)(2,1)S(1)}, u32[]{:S(2)}, u32[]{:S(2)}) %collective-permute-start.10) | collective-permute-done | bytes 1638432 | tf_op jit(solution)/shard_map/ppermute | solution.py:83
  77.0 2.4 collective-permute-start.12
  82.2 3.0 fusion.15
  85.1 8.8 %broadcast_in_dim.73 = bf16[5120,2560]{1,0:T(8,128)(2,1)} broadcast(bf16[]{:T(256)} %constant.238.clone.1), dimensions={} | broadcast | bytes 26214402 | tf_op jit(solution)/shard_map/broadcast_in_dim | solution.py:78
  96.7 2.1 collective-permute-start.13
  106.0 4.3 %select_bitcast_fusion.2 = (bf16[2,512,512]{2,1,0:T(8,128)(2,1)}, bf16[2,512,512]{2,1,0:T(8,128)(2,1)}) fusion(bf16[4,2,512,512]{3,2,1,0:T(8,128)(2,1)} %param.15, s32[]{:T(128)S(6)} %select_n.367, pred[]{:T(512)} %get-tuple-element.77, s32[]{:T(128)S(6)} %select_n.359, pred[]{:T(512)} %get-tuple-element.92), kind=kLoop, calls=%fused_computation.48 | loop fusion | flops 1048576 | bytes 4194314 | tf_op jit(solution)/shard_map/jit(_where)/select_n | solution.py:109
  110.4 5.5 %collective-permute-start.1 = (bf16[2,512,512]{2,1,0:T(8,128)(2,1)}, bf16[2,512,512]{2,1,0:T(8,128)(2,1)}, u32[]{:S(2)}, u32[]{:S(2)}) collective-permute-start(bf16[2,512,512]{2,1,0:T(8,128)(2,1)} %get-tuple-element.89), channel_id=1, source_target_pairs={{2,0},{3,1},{4,2},{5,3},{6,4},{7,5},{8,6},{9,7},{10,8},{11,9},{12,... | collective-permute-start | bytes 3145736 | tf_op jit(solution)/shard_map/ppermute | solution.py:19
  118.1 27.5 %collective-permute-done.13 = bf16[320,2560]{1,0:T(8,128)(2,1)} collective-permute-done((bf16[320,2560]{1,0:T(8,128)(2,1)}, bf16[320,2560]{1,0:T(8,128)(2,1)}, u32[]{:S(2)}, u32[]{:S(2)}) %collective-permute-start.13) | collective-permute-done | bytes 1638432 | tf_op jit(solution)/shard_map/ppermute | solution.py:88
  150.5 35.1 %collective-permute-done.14 = bf16[320,2560]{1,0:T(8,128)(2,1)} collective-permute-done((bf16[320,2560]{1,0:T(8,128)(2,1)}, bf16[320,2560]{1,0:T(8,128)(2,1)}, u32[]{:S(2)}, u32[]{:S(2)}) %collective-permute-start.14) | collective-permute-done | bytes 1638432 | tf_op jit(solution)/shard_map/ppermute | solution.py:83
  185.6 2.5 collective-permute-start.16
  188.1 2.2 bitcast_dynamic-update-slice_fusion.3
  190.3 2.3 bitcast_dynamic-update-slice_fusion.2
  192.6 3.8 select_bitcast_fusion
  196.9 2.7 constant_dynamic-update-slice_fusion.15
  199.6 38.1 %collective-permute-done.15 = bf16[320,2560]{1,0:T(8,128)(2,1)} collective-permute-done((bf16[320,2560]{1,0:T(8,128)(2,1)}, bf16[320,2560]{1,0:T(8,128)(2,1)}, u32[]{:S(2)}, u32[]{:S(2)}) %collective-permute-start.15) | collective-permute-done | bytes 1638432 | tf_op jit(solution)/shard_map/ppermute | solution.py:88
  240.7 5.7 %collective-permute-done.5 = bf16[2,512,512]{2,1,0:T(8,128)(2,1)} collective-permute-done((bf16[2,512,512]{2,1,0:T(8,128)(2,1)}, bf16[2,512,512]{2,1,0:T(8,128)(2,1)}, u32[]{:S(2)}, u32[]{:S(2)}) %collective-permute-start.5) | collective-permute-done | bytes 1048608 | tf_op jit(solution)/shard_map/ppermute | solution.py:19
  246.5 2.3 bitcast_dynamic-update-slice_fusion.1
  248.8 8.9 %collective-permute-done.7 = bf16[2,512,512]{2,1,0:T(8,128)(2,1)S(1)} collective-permute-done((bf16[2,512,512]{2,1,0:T(8,128)(2,1)}, bf16[2,512,512]{2,1,0:T(8,128)(2,1)S(1)}, u32[]{:S(2)}, u32[]{:S(2)}) %collective-permute-start.7) | collective-permute-done | bytes 1048608 | tf_op jit(solution)/shard_map/ppermute | solution.py:19
  258.7 5.3 %gather_fusion.6 = bf16[4,2,512,512]{3,2,1,0:T(8,128)(2,1)} fusion(bf16[5,2,512,512]{3,2,1,0:T(8,128)(2,1)} %bitcast_dynamic-update-slice_fusion, s32[1024]{0:T(1024)S(1)} %pad_clamp_fusion), kind=kCustom, calls=%fused_computation.6 | custom fusion | bytes 8388624 | tf_op jit(solution)/shard_map/jit(_take)/gather | solution.py:121
  264.0 4.7 %broadcast_select_fusion = bf16[2,2,2,512,512]{4,3,2,1,0:T(8,128)(2,1)} fusion(bf16[2,2,2,512,512]{4,3,2,1,0:T(8,128)(2,1)} %bitcast.95, pred[2,2]{1,0:T(4,128)(4,1)S(1)} %compare_and_fusion.1), kind=kLoop, calls=%fused_computation.38 | loop fusion | flops 2097152 | bytes 8388612 | tf_op jit(solution)/shard_map/jit(_take)/select_n | solution.py:121
  270.1 6.0 %collective-permute-done.17 = bf16[320,2560]{1,0:T(8,128)(2,1)} collective-permute-done((bf16[320,2560]{1,0:T(8,128)(2,1)}, bf16[320,2560]{1,0:T(8,128)(2,1)}, u32[]{:S(2)}, u32[]{:S(2)}) %collective-permute-start.17) | collective-permute-done | bytes 1638432 | tf_op jit(solution)/shard_map/ppermute | solution.py:88
  276.1 2.8 constant_dynamic-update-slice_fusion.12
  278.8 14.0 %collective-permute-done.18 = bf16[320,2560]{1,0:T(8,128)(2,1)S(1)} collective-permute-done((bf16[320,2560]{1,0:T(8,128)(2,1)}, bf16[320,2560]{1,0:T(8,128)(2,1)S(1)}, u32[]{:S(2)}, u32[]{:S(2)}) %collective-permute-start.18) | collective-permute-done | bytes 1638432 | tf_op jit(solution)/shard_map/ppermute | solution.py:83
  292.8 2.4 collective-permute-start.20
  295.2 2.7 constant_dynamic-update-slice_fusion.11
  297.9 2.7 constant_dynamic-update-slice_fusion.10
  300.6 2.7 constant_dynamic-update-slice_fusion.9
  303.3 2.8 constant_dynamic-update-slice_fusion.8
  306.1 8.3 %collective-permute-done.19 = bf16[320,2560]{1,0:T(8,128)(2,1)S(1)} collective-permute-done((bf16[320,2560]{1,0:T(8,128)(2,1)}, bf16[320,2560]{1,0:T(8,128)(2,1)S(1)}, u32[]{:S(2)}, u32[]{:S(2)}) %collective-permute-start.19) | collective-permute-done | bytes 1638432 | tf_op jit(solution)/shard_map/ppermute | solution.py:88
  314.4 2.7 constant_dynamic-update-slice_fusion.7
  317.1 13.7 %collective-permute-done.20 = bf16[320,2560]{1,0:T(8,128)(2,1)S(1)} collective-permute-done((bf16[320,2560]{1,0:T(8,128)(2,1)S(1)}, bf16[320,2560]{1,0:T(8,128)(2,1)S(1)}, u32[]{:S(2)}, u32[]{:S(2)}) %collective-permute-start.20) | collective-permute-done | bytes 1638432 | tf_op jit(solution)/shard_map/ppermute | solution.py:83
  330.8 2.5 collective-permute-start.22
  333.3 2.7 constant_dynamic-update-slice_fusion.6
  339.9 12.6 %collective-permute-done.21 = bf16[320,2560]{1,0:T(8,128)(2,1)S(1)} collective-permute-done((bf16[320,2560]{1,0:T(8,128)(2,1)S(1)}, bf16[320,2560]{1,0:T(8,128)(2,1)S(1)}, u32[]{:S(2)}, u32[]{:S(2)}) %collective-permute-start.21) | collective-permute-done | bytes 1638432 | tf_op jit(solution)/shard_map/ppermute | solution.py:88
  355.1 15.6 %fusion.18 = bf16[384,2560]{1,0:T(8,128)(2,1)} fusion(bf16[5120,2560]{1,0:T(8,128)(2,1)} %constant_dynamic-update-slice_fusion.1, bf16[384,5120]{1,0:T(8,128)(2,1)S(1)} %copy-done.4, f32[5120]{0:T(1024)S(1)} %copy-done.7, f32[384]{0:T(512)S(1)} %add_rsqrt_fusion, f32[2560]{0:T(1024)S(1)} %copy-done.8), kind=kOutput, calls=%fused_computation.37 | convolution fusion | flops 10076160000 | bytes 32144896 | tf_op jit(solution)/shard_map/dot_general | solution.py:96
  370.7 57.3 %while.10 = (s32[]{:T(128)}, bf16[2,192,2560]{2,1,0:T(8,128)(2,1)}, s32[2]{0:T(128)S(1)}, bf16[2,2,2,512,512]{4,3,2,1,0:T(8,128)(2,1)}, s32[2,2]{1,0:T(2,128)S(1...) while((s32[]{:T(128)}, bf16[2,192,2560]{2,1,0:T(8,128)(2,1)}, s32[2]{0:T(128)S(1)}, ...), condition=%wide.region_14.15_spmd, body=%wide.region_11.14_spmd.sunk | while | flops 2057990912 | bytes 138627664 | solution.py:63
  376.1 2.2 constant_dynamic-slice_fusion.7
  379.9 3.0 bitcast_reduce_fusion.2
  382.9 4.1 fusion.48
  388.7 7.5 %bitcast_divide_fusion.2 = bf16[192,4,5,128]{3,0,2,1:T(8,128)(2,1)S(1)} fusion(f32[4,1024,192,5]{1,2,3,0:T(8,128)} %copy-done.2, f32[192,4,5]{0,2,1:T(8,128)S(1)} %get-tuple-element.145, pred[1024]{0:T(1024)(128)(4,1)S(1)} %and.255, bf16[1024,4,128,1]{2,1,0,3:T(4,128)(2,1)S(1)} %bitcast.94, f32[192,4,5]{0,2,1:T(8,128)S(1)} %fusion.48), kind=kOutput, calls=%fused_computation.17.clone.1 | convolution fusion | flops 1023344640 | bytes 17792000 | tf_op jit(solution)/shard_map/while/body/eval_jaxpr/rkgt,tkd->rkgd/dot_general | solution.py:51
  404.8 2.2 constant_dynamic-slice_fusion.7
  408.6 3.0 bitcast_reduce_fusion.2
  411.5 4.1 fusion.48
  417.3 7.5 %bitcast_divide_fusion.2 = bf16[192,4,5,128]{3,0,2,1:T(8,128)(2,1)S(1)} fusion(f32[4,1024,192,5]{1,2,3,0:T(8,128)} %copy-done.2, f32[192,4,5]{0,2,1:T(8,128)S(1)} %get-tuple-element.145, pred[1024]{0:T(1024)(128)(4,1)S(1)} %and.255, bf16[1024,4,128,1]{2,1,0,3:T(4,128)(2,1)S(1)} %bitcast.94, f32[192,4,5]{0,2,1:T(8,128)S(1)} %fusion.48), kind=kOutput, calls=%fused_computation.17.clone.1 | convolution fusion | flops 1023344640 | bytes 17792000 | tf_op jit(solution)/shard_map/while/body/eval_jaxpr/rkgt,tkd->rkgd/dot_general | solution.py:51
  (127 shorter events, 48.6 us)
Async XLA Ops:
  0.0 43.3 %copy-start = (s32[64]{0:T(128)S(1)}, s32[64]{0:T(128)}, u32[]{:S(2)}) copy-start(s32[64]{0:T(128)} %param.16) | copy-start | bytes 772
  0.0 38.6 %collective-permute-start.8 = (bf16[320,2560]{1,0:T(8,128)(2,1)}, bf16[320,2560]{1,0:T(8,128)(2,1)}, u32[]{:S(2)}, u32[]{:S(2)}) collective-permute-start(bf16[320,2560]{1,0:T(8,128)(2,1)} %param.13), channel_id=1, source_target_pairs={{0,1},{1,2},{2,3},{3,4},{4,5},{5,6},{6,7},{7,8},{8,9},{9,10},{10,1... | collective-permute-start | bytes 4915208 | tf_op jit(solution)/shard_map/ppermute | solution.py:83
  2.6 55.9 %collective-permute-start.9 = (bf16[320,2560]{1,0:T(8,128)(2,1)}, bf16[320,2560]{1,0:T(8,128)(2,1)S(1)}, u32[]{:S(2)}, u32[]{:S(2)}) collective-permute-start(bf16[320,2560]{1,0:T(8,128)(2,1)} %param.13), channel_id=1, source_target_pairs={{0,15},{1,0},{2,1},{3,2},{4,3},{5,4},{6,5},{7,6},{8,7},{9,8},{10,9... | collective-permute-start | bytes 4915208 | tf_op jit(solution)/shard_map/ppermute | solution.py:88
  38.6 38.4 %collective-permute-start.10 = (bf16[320,2560]{1,0:T(8,128)(2,1)}, bf16[320,2560]{1,0:T(8,128)(2,1)S(1)}, u32[]{:S(2)}, u32[]{:S(2)}) collective-permute-start(bf16[320,2560]{1,0:T(8,128)(2,1)} %collective-permute-done.8), channel_id=1, source_target_pairs={{0,1},{1,2},{2,3},{3,4},{4,5},{5,6},{6,7},{7,8},{8,9},{9,10},{10,1... | collective-permute-start | bytes 4915208 | tf_op jit(solution)/shard_map/ppermute | solution.py:83
  41.0 54.1 %collective-permute-start = (s32[2,2]{1,0:T(2,128)}, s32[2,2]{1,0:T(2,128)S(1)}, u32[]{:S(2)}, u32[]{:S(2)}) collective-permute-start(s32[2,2]{1,0:T(2,128)} %param.17), channel_id=1, source_target_pairs={{14,0},{15,1},{0,2},{1,3},{2,4},{3,5},{4,6},{5,7},{6,8},{7,9},{8,1... | collective-permute-start | bytes 56 | tf_op jit(solution)/shard_map/ppermute | solution.py:19
  41.1 54.2 %collective-permute-start.2 = (s32[2,2]{1,0:T(2,128)}, s32[2,2]{1,0:T(2,128)S(1)}, u32[]{:S(2)}, u32[]{:S(2)}) collective-permute-start(s32[2,2]{1,0:T(2,128)} %param.17), channel_id=1, source_target_pairs={{15,0},{0,1},{1,2},{2,3},{3,4},{4,5},{5,6},{6,7},{7,8},{8,9},{9,10... | collective-permute-start | bytes 56 | tf_op jit(solution)/shard_map/ppermute | solution.py:19
  41.7 74.2 %collective-permute-start.4 = (s32[2,2]{1,0:T(2,128)}, s32[2,2]{1,0:T(2,128)S(1)}, u32[]{:S(2)}, u32[]{:S(2)}) collective-permute-start(s32[2,2]{1,0:T(2,128)} %param.17), channel_id=1, source_target_pairs={{1,0},{2,1},{3,2},{4,3},{5,4},{6,5},{7,6},{8,7},{9,8},{10,9},{11,1... | collective-permute-start | bytes 56 | tf_op jit(solution)/shard_map/ppermute | solution.py:19
  58.5 38.2 %collective-permute-start.11 = (bf16[320,2560]{1,0:T(8,128)(2,1)S(1)}, bf16[320,2560]{1,0:T(8,128)(2,1)}, u32[]{:S(2)}, u32[]{:S(2)}) collective-permute-start(bf16[320,2560]{1,0:T(8,128)(2,1)S(1)} %collective-permute-done.9), channel_id=1, source_target_pairs={{0,15},{1,0},{2,1},{3,2},{4,3},{5,4},{6,5},{7,6},{8,7},{9,8},{10,9... | collective-permute-start | bytes 4915208 | tf_op jit(solution)/shard_map/ppermute | solution.py:88
  77.0 23.1 %collective-permute-start.12 = (bf16[320,2560]{1,0:T(8,128)(2,1)S(1)}, bf16[320,2560]{1,0:T(8,128)(2,1)}, u32[]{:S(2)}, u32[]{:S(2)}) collective-permute-start(bf16[320,2560]{1,0:T(8,128)(2,1)S(1)} %collective-permute-done.10), channel_id=1, source_target_pairs={{0,1},{1,2},{2,3},{3,4},{4,5},{5,6},{6,7},{7,8},{8,9},{9,10},{10,1... | collective-permute-start | bytes 4915208 | tf_op jit(solution)/shard_map/ppermute | solution.py:83
  85.1 8.8 %copy-start.5 = (bf16[320,2560]{1,0:T(8,128)(2,1)S(1)}, bf16[320,2560]{1,0:T(8,128)(2,1)}, u32[]{:S(2)}) copy-start(bf16[320,2560]{1,0:T(8,128)(2,1)} %param.13) | copy-start | bytes 4915204
  85.1 10.1 %copy-start.6 = (s32[2,2]{1,0:T(2,128)S(1)}, s32[2,2]{1,0:T(2,128)}, u32[]{:S(2)}) copy-start(s32[2,2]{1,0:T(2,128)} %param.17) | copy-start | bytes 52
  95.2 21.5 %collective-permute-start.6 = (s32[2,2]{1,0:T(2,128)S(1)}, s32[2,2]{1,0:T(2,128)S(1)}, u32[]{:S(2)}, u32[]{:S(2)}) collective-permute-start(s32[2,2]{1,0:T(2,128)S(1)} %copy-done.6), channel_id=1, source_target_pairs={{2,0},{3,1},{4,2},{5,3},{6,4},{7,5},{8,6},{9,7},{10,8},{11,9},{12,... | collective-permute-start | bytes 56 | tf_op jit(solution)/shard_map/ppermute | solution.py:19
  96.7 48.8 %collective-permute-start.13 = (bf16[320,2560]{1,0:T(8,128)(2,1)}, bf16[320,2560]{1,0:T(8,128)(2,1)}, u32[]{:S(2)}, u32[]{:S(2)}) collective-permute-start(bf16[320,2560]{1,0:T(8,128)(2,1)} %collective-permute-done.11), channel_id=1, source_target_pairs={{0,15},{1,0},{2,1},{3,2},{4,3},{5,4},{6,5},{7,6},{8,7},{9,8},{10,9... | collective-permute-start | bytes 4915208 | tf_op jit(solution)/shard_map/ppermute | solution.py:88
  100.1 85.4 %collective-permute-start.14 = (bf16[320,2560]{1,0:T(8,128)(2,1)}, bf16[320,2560]{1,0:T(8,128)(2,1)}, u32[]{:S(2)}, u32[]{:S(2)}) collective-permute-start(bf16[320,2560]{1,0:T(8,128)(2,1)} %collective-permute-done.12), channel_id=1, source_target_pairs={{0,1},{1,2},{2,3},{3,4},{4,5},{5,6},{6,7},{7,8},{8,9},{9,10},{10,1... | collective-permute-start | bytes 4915208 | tf_op jit(solution)/shard_map/ppermute | solution.py:83
  110.4 77.7 %collective-permute-start.1 = (bf16[2,512,512]{2,1,0:T(8,128)(2,1)}, bf16[2,512,512]{2,1,0:T(8,128)(2,1)}, u32[]{:S(2)}, u32[]{:S(2)}) collective-permute-start(bf16[2,512,512]{2,1,0:T(8,128)(2,1)} %get-tuple-element.89), channel_id=1, source_target_pairs={{2,0},{3,1},{4,2},{5,3},{6,4},{7,5},{8,6},{9,7},{10,8},{11,9},{12,... | collective-permute-start | bytes 3145736 | tf_op jit(solution)/shard_map/ppermute | solution.py:19
  115.9 74.4 %collective-permute-start.3 = (bf16[2,512,512]{2,1,0:T(8,128)(2,1)}, bf16[2,512,512]{2,1,0:T(8,128)(2,1)}, u32[]{:S(2)}, u32[]{:S(2)}) collective-permute-start(bf16[2,512,512]{2,1,0:T(8,128)(2,1)} %get-tuple-element.88), channel_id=1, source_target_pairs={{1,0},{2,1},{3,2},{4,3},{5,4},{6,5},{7,6},{8,7},{9,8},{10,9},{11,1... | collective-permute-start | bytes 3145736 | tf_op jit(solution)/shard_map/ppermute | solution.py:19
  145.6 92.1 %collective-permute-start.15 = (bf16[320,2560]{1,0:T(8,128)(2,1)}, bf16[320,2560]{1,0:T(8,128)(2,1)}, u32[]{:S(2)}, u32[]{:S(2)}) collective-permute-start(bf16[320,2560]{1,0:T(8,128)(2,1)} %collective-permute-done.13), channel_id=1, source_target_pairs={{0,15},{1,0},{2,1},{3,2},{4,3},{5,4},{6,5},{7,6},{8,7},{9,8},{10,9... | collective-permute-start | bytes 4915208 | tf_op jit(solution)/shard_map/ppermute | solution.py:88
  150.5 42.1 %copy-start.3 = (bf16[4,2,512,512]{3,2,1,0:T(8,128)(2,1)S(1)}, bf16[4,2,512,512]{3,2,1,0:T(8,128)(2,1)}, u32[]{:S(2)}) copy-start(bf16[4,2,512,512]{3,2,1,0:T(8,128)(2,1)} %param.15) | copy-start | bytes 12582916
  185.6 53.4 %collective-permute-start.16 = (bf16[320,2560]{1,0:T(8,128)(2,1)}, bf16[320,2560]{1,0:T(8,128)(2,1)}, u32[]{:S(2)}, u32[]{:S(2)}) collective-permute-start(bf16[320,2560]{1,0:T(8,128)(2,1)} %collective-permute-done.14), channel_id=1, source_target_pairs={{0,1},{1,2},{2,3},{3,4},{4,5},{5,6},{6,7},{7,8},{8,9},{9,10},{10,1... | collective-permute-start | bytes 4915208 | tf_op jit(solution)/shard_map/ppermute | solution.py:83
  196.3 50.1 %collective-permute-start.5 = (bf16[2,512,512]{2,1,0:T(8,128)(2,1)}, bf16[2,512,512]{2,1,0:T(8,128)(2,1)}, u32[]{:S(2)}, u32[]{:S(2)}) collective-permute-start(bf16[2,512,512]{2,1,0:T(8,128)(2,1)} %get-tuple-element.87), channel_id=1, source_target_pairs={{15,0},{0,1},{1,2},{2,3},{3,4},{4,5},{5,6},{6,7},{7,8},{8,9},{9,10... | collective-permute-start | bytes 3145736 | tf_op jit(solution)/shard_map/ppermute | solution.py:19
  196.7 61.0 %collective-permute-start.7 = (bf16[2,512,512]{2,1,0:T(8,128)(2,1)}, bf16[2,512,512]{2,1,0:T(8,128)(2,1)S(1)}, u32[]{:S(2)}, u32[]{:S(2)}) collective-permute-start(bf16[2,512,512]{2,1,0:T(8,128)(2,1)} %get-tuple-element.85), channel_id=1, source_target_pairs={{14,0},{15,1},{0,2},{1,3},{2,4},{3,5},{4,6},{5,7},{6,8},{7,9},{8,1... | collective-permute-start | bytes 3145736 | tf_op jit(solution)/shard_map/ppermute | solution.py:19
  237.7 38.4 %collective-permute-start.17 = (bf16[320,2560]{1,0:T(8,128)(2,1)}, bf16[320,2560]{1,0:T(8,128)(2,1)}, u32[]{:S(2)}, u32[]{:S(2)}) collective-permute-start(bf16[320,2560]{1,0:T(8,128)(2,1)} %collective-permute-done.15), channel_id=1, source_target_pairs={{0,15},{1,0},{2,1},{3,2},{4,3},{5,4},{6,5},{7,6},{8,7},{9,8},{10,9... | collective-permute-start | bytes 4915208 | tf_op jit(solution)/shard_map/ppermute | solution.py:88
  239.0 53.8 %collective-permute-start.18 = (bf16[320,2560]{1,0:T(8,128)(2,1)}, bf16[320,2560]{1,0:T(8,128)(2,1)S(1)}, u32[]{:S(2)}, u32[]{:S(2)}) collective-permute-start(bf16[320,2560]{1,0:T(8,128)(2,1)} %collective-permute-done.16), channel_id=1, source_target_pairs={{0,1},{1,2},{2,3},{3,4},{4,5},{5,6},{6,7},{7,8},{8,9},{9,10},{10,1... | collective-permute-start | bytes 4915208 | tf_op jit(solution)/shard_map/ppermute | solution.py:83
  276.1 38.3 %collective-permute-start.19 = (bf16[320,2560]{1,0:T(8,128)(2,1)}, bf16[320,2560]{1,0:T(8,128)(2,1)S(1)}, u32[]{:S(2)}, u32[]{:S(2)}) collective-permute-start(bf16[320,2560]{1,0:T(8,128)(2,1)} %collective-permute-done.17), channel_id=1, source_target_pairs={{0,15},{1,0},{2,1},{3,2},{4,3},{5,4},{6,5},{7,6},{8,7},{9,8},{10,9... | collective-permute-start | bytes 4915208 | tf_op jit(solution)/shard_map/ppermute | solution.py:88
  292.8 38.0 %collective-permute-start.20 = (bf16[320,2560]{1,0:T(8,128)(2,1)S(1)}, bf16[320,2560]{1,0:T(8,128)(2,1)S(1)}, u32[]{:S(2)}, u32[]{:S(2)}) collective-permute-start(bf16[320,2560]{1,0:T(8,128)(2,1)S(1)} %collective-permute-done.18), channel_id=1, source_target_pairs={{0,1},{1,2},{2,3},{3,4},{4,5},{5,6},{6,7},{7,8},{8,9},{9,10},{10,1... | collective-permute-start | bytes 4915208 | tf_op jit(solution)/shard_map/ppermute | solution.py:83
  314.4 38.1 %collective-permute-start.21 = (bf16[320,2560]{1,0:T(8,128)(2,1)S(1)}, bf16[320,2560]{1,0:T(8,128)(2,1)S(1)}, u32[]{:S(2)}, u32[]{:S(2)}) collective-permute-start(bf16[320,2560]{1,0:T(8,128)(2,1)S(1)} %collective-permute-done.19), channel_id=1, source_target_pairs={{0,15},{1,0},{2,1},{3,2},{4,3},{5,4},{6,5},{7,6},{8,7},{9,8},{10,9... | collective-permute-start | bytes 4915208 | tf_op jit(solution)/shard_map/ppermute | solution.py:88
  330.8 23.0 %collective-permute-start.22 = (bf16[320,2560]{1,0:T(8,128)(2,1)S(1)}, bf16[320,2560]{1,0:T(8,128)(2,1)S(1)}, u32[]{:S(2)}, u32[]{:S(2)}) collective-permute-start(bf16[320,2560]{1,0:T(8,128)(2,1)S(1)} %collective-permute-done.20), channel_id=1, source_target_pairs={{0,1},{1,2},{2,3},{3,4},{4,5},{5,6},{6,7},{7,8},{8,9},{9,10},{10,1... | collective-permute-start | bytes 4915208 | tf_op jit(solution)/shard_map/ppermute | solution.py:83
  338.6 16.5 %copy-start.4 = (bf16[384,5120]{1,0:T(8,128)(2,1)S(1)}, bf16[384,5120]{1,0:T(8,128)(2,1)}, u32[]{:S(2)}) copy-start(bf16[384,5120]{1,0:T(8,128)(2,1)} %param.11) | copy-start | bytes 11796484
  338.6 16.5 %copy-start.7 = (f32[5120]{0:T(1024)S(1)}, f32[5120]{0:T(1024)}, u32[]{:S(2)}) copy-start(f32[5120]{0:T(1024)} %param.12) | copy-start | bytes 61444
  338.6 16.5 %copy-start.8 = (f32[2560]{0:T(1024)S(1)}, f32[2560]{0:T(1024)}, u32[]{:S(2)}) copy-start(f32[2560]{0:T(1024)} %param.14) | copy-start | bytes 30724
  355.1 15.6 %copy-start.9 = (s32[2]{0:T(128)S(1)}, s32[2]{0:T(128)}, u32[]{:S(2)}) copy-start(s32[2]{0:T(128)} %param.19) | copy-start | bytes 28
  355.1 15.6 %copy-start.10 = (s32[2]{0:T(128)S(1)}, s32[2]{0:T(128)}, u32[]{:S(2)}) copy-start(s32[2]{0:T(128)} %param.18) | copy-start | bytes 28
  382.9 5.5 %copy-start.2 = (f32[4,1024,192,5]{1,2,3,0:T(8,128)}, f32[4,1024,192,5]{1,2,3,0:T(8,128)S(1)}, u32[]{:S(2)}) copy-start(f32[4,1024,192,5]{1,2,3,0:T(8,128)S(1)} %get-tuple-element.144) | copy-start | bytes 47185924 | tf_op jit(solution)/shard_map/while
  411.5 5.5 %copy-start.2 = (f32[4,1024,192,5]{1,2,3,0:T(8,128)}, f32[4,1024,192,5]{1,2,3,0:T(8,128)S(1)}, u32[]{:S(2)}) copy-start(f32[4,1024,192,5]{1,2,3,0:T(8,128)S(1)} %get-tuple-element.144) | copy-start | bytes 47185924 | tf_op jit(solution)/shard_map/while
  428.0 0.7 copy-start.1
